TPU v7x, 32 devices: a whole 2x2x4 slice. The times are simulated.
32 devices in a mesh: gx: 8 (over z, y), gz: 4 (over x, core).
Axes of the slice: x: 2, y: 2, z: 4, core: 2. Of those that a mesh axis runs over, the one named last changes fastest.
Arguments:
- field: float32 [4, 4, 512, 1024], P(None, 'gz', None, 'gx'), may hold values from -6 to 6
- drop_cell: int32 [131072], P(('gx', 'gz')), may hold values from 0 to 65535
- drop_plane: int32 [131072], P(('gx', 'gz')), may hold values from 0 to 3
- drop_rate: float32 [2, 131072], P(None, ('gx', 'gz')), may hold values from -8 to 8
- diffusivity: float32 [4], replicated, may hold values from 0.25 to 4
- wall_eigen: float32 [512], replicated, may hold values from 0.05 to 2
- basis_part: float32 [512, 512], replicated, may hold values from -0.125 to 0.125
- dual_part: float32 [512, 512], replicated, may hold values from -0.125 to 0.125
- bulk_shift: float32 [1], replicated, may hold values from 2.2 to 2.8
Outputs:
- new_field: float32 [4, 4, 512, 1024], P(None, 'gz', None, 'gx')
All inputs are finite; a program needn't handle non-finite values.
Results may differ from a plain program's by a relative error of at most 0.0001.
Values sent between devices are 32-bit elements; how exact they have to be, the bound alone decides.
A program may use at most 64 MiB of HBM per device.

v0:
```python
import math

import jax
import jax.numpy as jnp
from jax import lax
from jax.sharding import PartitionSpec as P


def partner(array, axis, apart):
    return lax.ppermute(array, axis, [(i, i ^ 1 << apart) for i in range(lax.axis_size(axis))])


def phase_tables(length):
    counter = jnp.arange(length, dtype=jnp.int32)
    product = counter[:, None] * counter[None, :] % length
    angle = 2.0 * math.pi / length * product.astype(jnp.float32)
    return (jnp.cos(angle), jnp.sin(angle))


def along_last(values, table):
    return jnp.einsum("fzyj,jm->fzym", values, table, precision=lax.Precision.HIGHEST)


def crank_factor(diffusivity, eigen_rows, mode_index, total_cells):
    folded = jnp.minimum(mode_index, total_cells - mode_index).astype(jnp.float32)
    wavenumber = 2.0 * math.pi / total_cells * folded
    growth = diffusivity[:, None, None] * (
        eigen_rows[None, :, None] + wavenumber[None, None, :] ** 2
    )
    return (1.0 - growth) / (1.0 + growth)


def travel_phase(bulk_shift, mode_index, total_cells):
    signed = jnp.where(2 * mode_index >= total_cells, mode_index - total_cells, mode_index).astype(
        jnp.float32
    )
    travel = 2.0 * math.pi / total_cells * signed * bulk_shift[0]
    return (jnp.cos(travel), jnp.sin(travel))


def turn_modes(spec_real, spec_imag, damping, cos_travel, sin_travel):
    new_real = damping * (spec_real * cos_travel + spec_imag * sin_travel)
    new_imag = damping * (spec_imag * cos_travel - spec_real * sin_travel)
    return (new_real, new_imag)


def per_device(
    field,
    drop_cell,
    drop_plane,
    drop_rate,
    diffusivity,
    wall_eigen,
    basis_part,
    dual_part,
    bulk_shift,
):
    field_count, plane_count, row_count, slab_width = field.shape
    gx_count = lax.axis_size("gx")
    gz_count = lax.axis_size("gz")
    total_cells = slab_width * gx_count
    plane_cells = row_count * slab_width
    flat_cell = drop_plane * plane_cells + drop_cell
    partial_value = jnp.stack(
        [
            jax.ops.segment_sum(
                drop_rate[component], flat_cell, num_segments=plane_count * gz_count * plane_cells
            )
            for component in range(2)
        ]
    )
    partial_value = partial_value.reshape(2, plane_count * gz_count, row_count, slab_width)
    source = lax.psum_scatter(partial_value, "gz", scatter_dimension=1, tiled=True)
    right_side = jnp.concatenate([field[:2], field[2:] + source], axis=0)
    identity = jnp.eye(row_count, dtype=jnp.float32)
    projected = jnp.einsum(
        "ay,fzyx->fzax", identity + dual_part, right_side, precision=lax.Precision.HIGHEST
    )
    position = lax.axis_index("gx")
    bit_total = gx_count.bit_length() - 1
    real_part = projected
    imag_part = jnp.zeros_like(projected)
    for section_bit in range(bit_total - 1, -1, -1):
        half_span = 1 << section_bit
        other_real, other_imag = partner((real_part, imag_part), "gx", section_bit)
        upper_side = position // half_span % 2 == 1
        angle = -math.pi / half_span * (position % half_span).astype(jnp.float32)
        cosine = jnp.cos(angle)
        sine = jnp.sin(angle)
        diff_real = other_real - real_part
        diff_imag = other_imag - imag_part
        new_real = jnp.where(
            upper_side, diff_real * cosine - diff_imag * sine, real_part + other_real
        )
        new_imag = jnp.where(
            upper_side, diff_real * sine + diff_imag * cosine, imag_part + other_imag
        )
        real_part, imag_part = (new_real, new_imag)
    reversed_index = jnp.zeros((), jnp.int32)
    for bit_number in range(bit_total):
        reversed_index = reversed_index + position // (1 << bit_number) % 2 * (
            1 << bit_total - 1 - bit_number
        )
    columns = jnp.arange(slab_width, dtype=jnp.int32)
    twist = (
        2.0 * math.pi / total_cells * (reversed_index * columns % total_cells).astype(jnp.float32)
    )
    cos_twist = jnp.cos(twist)
    sin_twist = jnp.sin(twist)
    shifted_real = real_part * cos_twist + imag_part * sin_twist
    shifted_imag = imag_part * cos_twist - real_part * sin_twist
    cos_table, sin_table = phase_tables(slab_width)
    spec_real = along_last(shifted_real, cos_table) + along_last(shifted_imag, sin_table)
    spec_imag = along_last(shifted_imag, cos_table) - along_last(shifted_real, sin_table)
    mode_index = reversed_index + gx_count * columns
    damping = crank_factor(diffusivity, wall_eigen, mode_index, total_cells)[:, None]
    cos_travel, sin_travel = travel_phase(bulk_shift, mode_index, total_cells)
    spec_real, spec_imag = turn_modes(spec_real, spec_imag, damping, cos_travel, sin_travel)
    back_real = along_last(spec_real, cos_table) - along_last(spec_imag, sin_table)
    back_imag = along_last(spec_imag, cos_table) + along_last(spec_real, sin_table)
    real_part = back_real * cos_twist - back_imag * sin_twist
    imag_part = back_real * sin_twist + back_imag * cos_twist
    for section_bit in range(bit_total):
        half_span = 1 << section_bit
        other_real, other_imag = partner((real_part, imag_part), "gx", section_bit)
        upper_side = position // half_span % 2 == 1
        angle = math.pi / half_span * (position % half_span).astype(jnp.float32)
        cosine = jnp.cos(angle)
        sine = jnp.sin(angle)
        mine_real = real_part * cosine - imag_part * sine
        mine_imag = real_part * sine + imag_part * cosine
        turned_real = other_real * cosine - other_imag * sine
        turned_imag = other_real * sine + other_imag * cosine
        new_real = jnp.where(upper_side, other_real - mine_real, real_part + turned_real)
        new_imag = jnp.where(upper_side, other_imag - mine_imag, imag_part + turned_imag)
        real_part, imag_part = (new_real, new_imag)
    filtered = real_part / total_cells
    return jnp.einsum(
        "ya,fzax->fzyx", identity + basis_part, filtered, precision=lax.Precision.HIGHEST
    )


def solution(mesh):
    in_specs = (
        P(None, "gz", None, "gx"),
        P(("gx", "gz")),
        P(("gx", "gz")),
        P(None, ("gx", "gz")),
        P(),
        P(),
        P(),
        P(),
        P(),
    )
    out_specs = P(None, "gz", None, "gx")
    return jax.shard_map(
        per_device, mesh=mesh, in_specs=in_specs, out_specs=out_specs, check_vma=False
    )
```

profile of v0, /device:TPU:13, one launch (start us, length us, event | category | flops | bytes accessed | tf_op | source)
XLA Modules:
  0.0 461.1 jit_solution(2083587722057538931)
XLA Ops:
  6.5 0.9 fusion.105
  7.4 0.7 multiply_add_fusion.3
  8.1 22.2 %scatter_custom_fusion = f32[262144]{0:T(1024)S(1)} fusion(s32[4096]{0:T(1024)S(1)} %multiply_add_fusion.3, f32[4096]{0:T(1024)S(1)} %bitcast.72, f32[]{:T(128)} %constant.160.clone.1), kind=kCustom, calls=%fused_computation.60 | custom fusion | flops 4096 | bytes 1048580 | tf_op jit(solution)/shard_map/scatter-add | solution.py:66
  30.3 0.3 copy.23
  30.7 22.3 %scatter_custom_fusion.1 = f32[262144]{0:T(1024)S(1)} fusion(s32[4096]{0:T(1024)S(1)} %multiply_add_fusion.3, f32[4096]{0:T(1024)S(1)} %bitcast.71, f32[]{:T(128)} %constant.160.clone.1), kind=kCustom, calls=%fused_computation.58 | custom fusion | flops 4096 | bytes 1048580 | tf_op jit(solution)/shard_map/scatter-add | solution.py:66
  53.0 0.3 copy.24
  53.3 1.6 pad_maximum_fusion
  55.0 0.0 reduce-scatter.2.cloned.1.call-update
  55.0 1.1 broadcast_in_dim.5
  56.1 2.3 collective-permute-start.1
  58.4 0.0 copy-done.3
  58.4 0.1 fusion.104
  58.5 0.0 copy-start.1
  58.5 0.2 copy.43
  58.7 0.2 copy.42
  58.9 28.8 %reduce-scatter.2.cloned.1.call-done = f32[2,1,512,128]{2,3,0,1:T(8,128)} async-done(((f32[2,4,512,128]{2,3,0,1:T(8,128)}), f32[2,1,512,128]{2,3,0,1:T(8,128)}) %reduce-scatter.2.cloned.1.call-update) | async-done | bytes 524304 | tf_op jit(solution)/shard_map/reduce_scatter | solution.py:73
  87.7 1.1 add.217
  88.8 1.9 convolution_bitcast_fusion.1
  90.7 2.2 collective-permute-start
  93.1 33.4 %collective-permute-done.1 = f32[4,1,512,128]{2,3,0,1:T(8,128)} collective-permute-done((f32[4,1,512,128]{2,3,0,1:T(8,128)}, f32[4,1,512,128]{2,3,0,1:T(8,128)}, u32[]{:S(2)}, u32[]{:S(2)}) %collective-permute-start.1) | collective-permute-done | bytes 1048608 | tf_op jit(solution)/shard_map/ppermute | solution.py:10
  126.4 22.4 %collective-permute-done = f32[4,1,512,128]{2,3,0,1:T(8,128)} collective-permute-done((f32[4,1,512,128]{2,3,0,1:T(8,128)S(1)}, f32[4,1,512,128]{2,3,0,1:T(8,128)}, u32[]{:S(2)}, u32[]{:S(2)}) %collective-permute-start) | collective-permute-done | bytes 1048608 | tf_op jit(solution)/shard_map/ppermute | solution.py:10
  148.8 1.9 add_select_fusion.7
  150.8 0.2 collective-permute-start.2
  151.0 1.3 collective-permute-start.3
  152.5 0.0 copy-start.6
  152.5 22.6 %collective-permute-done.2 = f32[4,1,512,128]{2,3,0,1:T(8,128)S(1)} collective-permute-done((f32[4,1,512,128]{2,3,0,1:T(8,128)S(1)}, f32[4,1,512,128]{2,3,0,1:T(8,128)S(1)}, u32[]{:S(2)}, u32[]{:S(2)}) %collective-permute-start.2) | collective-permute-done | bytes 1048608 | tf_op jit(solution)/shard_map/ppermute | solution.py:10
  175.1 1.0 copy-done.4
  176.0 21.6 %collective-permute-done.3 = f32[4,1,512,128]{2,3,0,1:T(8,128)} collective-permute-done((f32[4,1,512,128]{2,3,0,1:T(8,128)S(1)}, f32[4,1,512,128]{2,3,0,1:T(8,128)}, u32[]{:S(2)}, u32[]{:S(2)}) %collective-permute-start.3) | collective-permute-done | bytes 1048608 | tf_op jit(solution)/shard_map/ppermute | solution.py:10
  197.6 2.4 add_select_fusion.5
  200.0 0.3 collective-permute-start.4
  200.3 1.3 collective-permute-start.5
  202.3 0.1 fusion.67
  202.3 0.1 fusion.62
  202.4 0.1 broadcast_add_fusion
  202.5 20.9 %collective-permute-done.4 = f32[4,1,512,128]{2,3,0,1:T(8,128)S(1)} collective-permute-done((f32[4,1,512,128]{2,3,0,1:T(8,128)S(1)}, f32[4,1,512,128]{2,3,0,1:T(8,128)S(1)}, u32[]{:S(2)}, u32[]{:S(2)}) %collective-permute-start.4) | collective-permute-done | bytes 1048608 | tf_op jit(solution)/shard_map/ppermute | solution.py:10
  223.4 1.0 copy-done.2
  224.4 21.6 %collective-permute-done.5 = f32[4,1,512,128]{2,3,0,1:T(8,128)} collective-permute-done((f32[4,1,512,128]{2,3,0,1:T(8,128)S(1)}, f32[4,1,512,128]{2,3,0,1:T(8,128)}, u32[]{:S(2)}, u32[]{:S(2)}) %collective-permute-start.5) | collective-permute-done | bytes 1048608 | tf_op jit(solution)/shard_map/ppermute | solution.py:10
  246.0 2.1 add_select_fusion.3
  248.0 2.1 fusion.14
  250.1 2.1 fusion.10
  252.2 2.1 convolution_add_fusion.1
  254.2 0.0 copy-start.7
  254.3 2.3 convolution_subtract_fusion.1
  256.6 1.7 fusion.41
  258.2 1.7 fusion.43
  259.9 1.7 convolution_subtract_fusion
  261.6 1.9 multiply_add_fusion.1
  263.5 0.3 collective-permute-start.6
  263.8 1.2 collective-permute-start.7
  265.0 20.9 %collective-permute-done.6 = f32[4,1,512,128]{2,3,0,1:T(8,128)S(1)} collective-permute-done((f32[4,1,512,128]{2,3,0,1:T(8,128)S(1)}, f32[4,1,512,128]{2,3,0,1:T(8,128)S(1)}, u32[]{:S(2)}, u32[]{:S(2)}) %collective-permute-start.6) | collective-permute-done | bytes 1048608 | tf_op jit(solution)/shard_map/ppermute | solution.py:10
  286.0 22.5 %collective-permute-done.7 = f32[4,1,512,128]{2,3,0,1:T(8,128)S(1)} collective-permute-done((f32[4,1,512,128]{2,3,0,1:T(8,128)S(1)}, f32[4,1,512,128]{2,3,0,1:T(8,128)S(1)}, u32[]{:S(2)}, u32[]{:S(2)}) %collective-permute-start.7) | collective-permute-done | bytes 1048608 | tf_op jit(solution)/shard_map/ppermute | solution.py:10
  308.4 0.5 fusion.8
  309.0 0.1 collective-permute-start.8
  309.0 1.5 collective-permute-start.9
  310.6 19.8 %collective-permute-done.8 = f32[4,1,512,128]{2,3,0,1:T(8,128)S(1)} collective-permute-done((f32[4,1,512,128]{2,3,0,1:T(8,128)S(1)}, f32[4,1,512,128]{2,3,0,1:T(8,128)S(1)}, u32[]{:S(2)}, u32[]{:S(2)}) %collective-permute-start.8) | collective-permute-done | bytes 1048608 | tf_op jit(solution)/shard_map/ppermute | solution.py:10
  330.5 1.0 copy-done.5
  331.5 21.6 %collective-permute-done.9 = f32[4,1,512,128]{2,3,0,1:T(8,128)} collective-permute-done((f32[4,1,512,128]{2,3,0,1:T(8,128)S(1)}, f32[4,1,512,128]{2,3,0,1:T(8,128)}, u32[]{:S(2)}, u32[]{:S(2)}) %collective-permute-start.9) | collective-permute-done | bytes 1048608 | tf_op jit(solution)/shard_map/ppermute | solution.py:10
  353.1 3.1 add_select_fusion
  356.2 3.2 collective-permute-start.10
  359.4 0.0 collective-permute-start.11
  359.6 66.9 %collective-permute-done.10 = f32[4,1,512,128]{2,3,0,1:T(8,128)S(1)} collective-permute-done((f32[4,1,512,128]{2,3,0,1:T(8,128)}, f32[4,1,512,128]{2,3,0,1:T(8,128)S(1)}, u32[]{:S(2)}, u32[]{:S(2)}) %collective-permute-start.10) | collective-permute-done | bytes 1048608 | tf_op jit(solution)/shard_map/ppermute | solution.py:10
  426.5 22.4 %collective-permute-done.11 = f32[4,1,512,128]{2,3,0,1:T(8,128)} collective-permute-done((f32[4,1,512,128]{2,3,0,1:T(8,128)S(1)}, f32[4,1,512,128]{2,3,0,1:T(8,128)}, u32[]{:S(2)}, u32[]{:S(2)}) %collective-permute-start.11) | collective-permute-done | bytes 1048608 | tf_op jit(solution)/shard_map/ppermute | solution.py:10
  448.8 4.1 convolution_bitcast_fusion
  452.9 1.3 copy.33
  (11 shorter events, 0.1 us)
Async XLA Ops:
  6.5 81.2 %reduce-scatter.2.cloned.1.call-start = ((), (), s32[]{:S(2)}) async-start(), calls=%async_computation.1 | async-start | bytes 2621440 | tf_op jit(solution)/shard_map/reduce_scatter | solution.py:73
  55.0 3.4 copy-start.3
  56.1 70.3 %collective-permute-start.1 = (f32[4,1,512,128]{2,3,0,1:T(8,128)}, f32[4,1,512,128]{2,3,0,1:T(8,128)}, u32[]{:S(2)}, u32[]{:S(2)}) collective-permute-start(f32[4,1,512,128]{2,3,0,1:T(8,128)} %broadcast_in_dim.5), channel_id=1, source_target_pairs={{0,16},{4,20},{8,24},{12,28},{16,0},{20,4},{24,8},{28,12},{1,17},{... | collective-permute-start | bytes 3145736 | tf_op jit(solution)/shard_map/ppermute | solution.py:10
  58.5 30.3 %copy-start.1 = (f32[512,512]{1,0:T(8,128)S(1)}, f32[512,512]{1,0:T(8,128)}, u32[]{:S(2)}) copy-start(f32[512,512]{1,0:T(8,128)} %param.16) | copy-start | bytes 3145732
  90.7 58.1 %collective-permute-start = (f32[4,1,512,128]{2,3,0,1:T(8,128)S(1)}, f32[4,1,512,128]{2,3,0,1:T(8,128)}, u32[]{:S(2)}, u32[]{:S(2)}) collective-permute-start(f32[4,1,512,128]{2,3,0,1:T(8,128)S(1)} %convolution_bitcast_fusion.1), channel_id=1, source_target_pairs={{0,16},{4,20},{8,24},{12,28},{16,0},{20,4},{24,8},{28,12},{1,17},{... | collective-permute-start | bytes 3145736 | tf_op jit(solution)/shard_map/ppermute | solution.py:10
  150.7 24.3 %copy-start = (f32[4,1,512,128]{2,3,0,1:T(8,128)}, f32[4,1,512,128]{2,3,0,1:T(8,128)S(1)}, u32[]{:S(2)}) copy-start(f32[4,1,512,128]{2,3,0,1:T(8,128)S(1)} %get-tuple-element.14) | copy-start | bytes 3145732
  150.8 24.3 %collective-permute-start.2 = (f32[4,1,512,128]{2,3,0,1:T(8,128)S(1)}, f32[4,1,512,128]{2,3,0,1:T(8,128)S(1)}, u32[]{:S(2)}, u32[]{:S(2)}) collective-permute-start(f32[4,1,512,128]{2,3,0,1:T(8,128)S(1)} %get-tuple-element.13), channel_id=1, source_target_pairs={{0,8},{4,12},{8,0},{12,4},{16,24},{20,28},{24,16},{28,20},{1,9},{5... | collective-permute-start | bytes 3145736 | tf_op jit(solution)/shard_map/ppermute | solution.py:10
  151.0 46.7 %collective-permute-start.3 = (f32[4,1,512,128]{2,3,0,1:T(8,128)S(1)}, f32[4,1,512,128]{2,3,0,1:T(8,128)}, u32[]{:S(2)}, u32[]{:S(2)}) collective-permute-start(f32[4,1,512,128]{2,3,0,1:T(8,128)S(1)} %get-tuple-element.14), channel_id=1, source_target_pairs={{0,8},{4,12},{8,0},{12,4},{16,24},{20,28},{24,16},{28,20},{1,9},{5... | collective-permute-start | bytes 3145736 | tf_op jit(solution)/shard_map/ppermute | solution.py:10
  152.5 49.9 %copy-start.6 = (f32[512]{0:T(512)S(1)}, f32[512]{0:T(512)}, u32[]{:S(2)}) copy-start(f32[512]{0:T(512)} %param.14) | copy-start | bytes 6148
  175.1 1.0 copy-start.4
  200.0 23.4 %collective-permute-start.4 = (f32[4,1,512,128]{2,3,0,1:T(8,128)S(1)}, f32[4,1,512,128]{2,3,0,1:T(8,128)S(1)}, u32[]{:S(2)}, u32[]{:S(2)}) collective-permute-start(f32[4,1,512,128]{2,3,0,1:T(8,128)S(1)} %get-tuple-element.11), channel_id=1, source_target_pairs={{0,4},{4,0},{8,12},{12,8},{16,20},{20,16},{24,28},{28,24},{1,5},{5... | collective-permute-start | bytes 3145736 | tf_op jit(solution)/shard_map/ppermute | solution.py:10
  200.3 45.7 %collective-permute-start.5 = (f32[4,1,512,128]{2,3,0,1:T(8,128)S(1)}, f32[4,1,512,128]{2,3,0,1:T(8,128)}, u32[]{:S(2)}, u32[]{:S(2)}) collective-permute-start(f32[4,1,512,128]{2,3,0,1:T(8,128)S(1)} %get-tuple-element.12), channel_id=1, source_target_pairs={{0,4},{4,0},{8,12},{12,8},{16,20},{20,16},{24,28},{28,24},{1,5},{5... | collective-permute-start | bytes 3145736 | tf_op jit(solution)/shard_map/ppermute | solution.py:10
  223.4 1.0 copy-start.2
  254.2 2.3 copy-start.7
  263.5 22.5 %collective-permute-start.6 = (f32[4,1,512,128]{2,3,0,1:T(8,128)S(1)}, f32[4,1,512,128]{2,3,0,1:T(8,128)S(1)}, u32[]{:S(2)}, u32[]{:S(2)}) collective-permute-start(f32[4,1,512,128]{2,3,0,1:T(8,128)S(1)} %bitcast.70), channel_id=1, source_target_pairs={{0,4},{4,0},{8,12},{12,8},{16,20},{20,16},{24,28},{28,24},{1,5},{5... | collective-permute-start | bytes 3145736 | tf_op jit(solution)/shard_map/ppermute | solution.py:10
  263.8 44.6 %collective-permute-start.7 = (f32[4,1,512,128]{2,3,0,1:T(8,128)S(1)}, f32[4,1,512,128]{2,3,0,1:T(8,128)S(1)}, u32[]{:S(2)}, u32[]{:S(2)}) collective-permute-start(f32[4,1,512,128]{2,3,0,1:T(8,128)S(1)} %bitcast.69), channel_id=1, source_target_pairs={{0,4},{4,0},{8,12},{12,8},{16,20},{20,16},{24,28},{28,24},{1,5},{5... | collective-permute-start | bytes 3145736 | tf_op jit(solution)/shard_map/ppermute | solution.py:10
  309.0 21.5 %collective-permute-start.8 = (f32[4,1,512,128]{2,3,0,1:T(8,128)S(1)}, f32[4,1,512,128]{2,3,0,1:T(8,128)S(1)}, u32[]{:S(2)}, u32[]{:S(2)}) collective-permute-start(f32[4,1,512,128]{2,3,0,1:T(8,128)S(1)} %get-tuple-element.8), channel_id=1, source_target_pairs={{0,8},{4,12},{8,0},{12,4},{16,24},{20,28},{24,16},{28,20},{1,9},{5... | collective-permute-start | bytes 3145736 | tf_op jit(solution)/shard_map/ppermute | solution.py:10
  309.0 44.0 %collective-permute-start.9 = (f32[4,1,512,128]{2,3,0,1:T(8,128)S(1)}, f32[4,1,512,128]{2,3,0,1:T(8,128)}, u32[]{:S(2)}, u32[]{:S(2)}) collective-permute-start(f32[4,1,512,128]{2,3,0,1:T(8,128)S(1)} %get-tuple-element.7), channel_id=1, source_target_pairs={{0,8},{4,12},{8,0},{12,4},{16,24},{20,28},{24,16},{28,20},{1,9},{5... | collective-permute-start | bytes 3145736 | tf_op jit(solution)/shard_map/ppermute | solution.py:10
  330.5 1.0 copy-start.5
  356.2 70.3 %collective-permute-start.10 = (f32[4,1,512,128]{2,3,0,1:T(8,128)}, f32[4,1,512,128]{2,3,0,1:T(8,128)S(1)}, u32[]{:S(2)}, u32[]{:S(2)}) collective-permute-start(f32[4,1,512,128]{2,3,0,1:T(8,128)} %get-tuple-element.6), channel_id=1, source_target_pairs={{0,16},{4,20},{8,24},{12,28},{16,0},{20,4},{24,8},{28,12},{1,17},{... | collective-permute-start | bytes 3145736 | tf_op jit(solution)/shard_map/ppermute | solution.py:10
  359.4 89.4 %collective-permute-start.11 = (f32[4,1,512,128]{2,3,0,1:T(8,128)S(1)}, f32[4,1,512,128]{2,3,0,1:T(8,128)}, u32[]{:S(2)}, u32[]{:S(2)}) collective-permute-start(f32[4,1,512,128]{2,3,0,1:T(8,128)S(1)} %get-tuple-element.5), channel_id=1, source_target_pairs={{0,16},{4,20},{8,24},{12,28},{16,0},{20,4},{24,8},{28,12},{1,17},{... | collective-permute-start | bytes 3145736 | tf_op jit(solution)/shard_map/ppermute | solution.py:10
Sparse Core Ops, SparseCore 0:
  55.1 32.5 reduce-scatter.1
where the time goes:
time: 466 us; the launch traced here: 461 us
  waiting for transfers between devices  345 us (74%)
  other arithmetic  58.3 us (13%)
  matrix products  21.3 us (5%)
  between operations  14.9 us (3%)
  starting transfers between devices  13.9 us (3%)
  local copies, waits for them, and re-layouts  7.33 us (2%)
    ppermute x12, waiting for transfers between devices, partner(): lax.ppermute(array, axis, [(i, i ^ 1 << apart) for i in range(lax.axis_si...  317 us
    scatter-add x2, other arithmetic, per_device(): jax.ops.segment_sum(drop_rate[component], flat_cell, num_segments=plane_c...  44.5 us
    reduce_scatter x1, waiting for transfers between devices, per_device(): lax.psum_scatter(partial_value, 'gz', scatter_dimension=1, tiled=True)  28.8 us
    dot_general x8, matrix products, along_last(): jnp.einsum('fzyj,jm->fzym', values, table, precision=lax.Precision.HIGHEST)  15.4 us
    ppermute x12, starting transfers between devices, partner(): lax.ppermute(array, axis, [(i, i ^ 1 << apart) for i in range(lax.axis_si...  13.9 us
  transfers between devices with their start and end apart: 13, of which 13 were waited for; matrix products, arithmetic and copies ran while one was open for 1% of the time, Pallas kernels for 0%

commit v1 on v0

v1 whole, which is shorter than its diff:
```python
import functools
import math

import jax
import jax.numpy as jnp
import numpy as np
from jax import lax
from jax.experimental import pallas as pl
from jax.experimental.pallas import tpu as pltpu
from jax.sharding import PartitionSpec as P

DENSE_LIMIT = 2048


def real_table(total):
    half = total // 2
    product = np.arange(total)[:, None] * np.arange(half)[None, :] % total
    angle = 2.0 * np.pi / total * product
    sines = -np.sin(angle)
    sines[:, 0] = 1.0 - 2.0 * (np.arange(total) % 2)
    return np.concatenate([np.cos(angle), sines], axis=1).astype(np.float32)


def deposit_kernel(slab_width, row_ref, col_ref, rate_ref, out_ref):
    rows = out_ref.shape[0]
    depth = row_ref.shape[1]

    @pl.when(pl.program_id(0) == 0)
    def _():
        out_ref[...] = jnp.zeros_like(out_ref)

    hit = lax.broadcasted_iota(jnp.int32, (rows, depth), 0) == row_ref[...]
    left = jnp.where(hit, 1.0, 0.0).astype(jnp.bfloat16)
    here = lax.broadcasted_iota(jnp.int32, (slab_width, depth), 0) == col_ref[...]
    terms = []
    for component in range(2):
        rate = rate_ref[component : component + 1, :]
        high = rate.astype(jnp.bfloat16).astype(jnp.float32)
        for part in (high, rate - high):
            terms.append(jnp.where(here, part, 0.0).astype(jnp.bfloat16))
    right = jnp.concatenate(terms, axis=0)
    out_ref[...] += lax.dot_general(
        left, right, (((1,), (1,)), ((), ())), preferred_element_type=jnp.float32
    )


def deposit(row, col, rate, row_count, slab_width):
    drops = row.shape[1]
    block = min(2048, drops)
    out = pl.pallas_call(
        functools.partial(deposit_kernel, slab_width),
        grid=(drops // block,),
        in_specs=[
            pl.BlockSpec((1, block), lambda i: (0, i)),
            pl.BlockSpec((1, block), lambda i: (0, i)),
            pl.BlockSpec((2, block), lambda i: (0, i)),
        ],
        out_specs=pl.BlockSpec((row_count, 4 * slab_width), lambda i: (0, 0)),
        out_shape=jax.ShapeDtypeStruct((row_count, 4 * slab_width), jnp.float32),
        compiler_params=pltpu.CompilerParams(vmem_limit_bytes=40 * 2**20),
    )(row, col, rate)
    parts = out.reshape(row_count, 2, 2, slab_width).sum(axis=2)
    return parts.transpose(1, 0, 2)


def damping_of(diffusivity, eigen_rows, mode_index, total_cells):
    wavenumber = 2.0 * math.pi / total_cells * mode_index.astype(jnp.float32)
    growth = diffusivity[:, None, None] * (
        eigen_rows[None, :, None] + wavenumber[None, None, :] ** 2
    )
    return (1.0 - growth) / (1.0 + growth)


def per_device(
    field, drop_cell, drop_plane, drop_rate, diffusivity, wall_eigen, basis_part, dual_part, bulk_shift
):
    field_count, _, row_count, slab_width = field.shape
    gx_count = lax.axis_size("gx")
    total = slab_width * gx_count
    own_rows = row_count // gx_count
    half = total // 2
    field = field[:, 0]
    drops = jnp.concatenate(
        [
            drop_cell.astype(jnp.float32)[None],
            drop_plane.astype(jnp.float32)[None],
            drop_rate,
        ]
    )
    drops = lax.all_gather(drops, "gz", axis=1, tiled=True)
    cell = drops[0].astype(jnp.int32)
    mine = drops[1].astype(jnp.int32) == lax.axis_index("gz")
    row = jnp.where(mine, cell // slab_width, -1)[None]
    col = (cell % slab_width)[None]
    source = deposit(row, col, drops[2:], row_count, slab_width)

    def project(matrix, values):
        return values + jnp.einsum("ay,fyx->fax", matrix, values, precision=lax.Precision.HIGH)

    def scatter_rows(values):
        pieces = values.reshape(values.shape[0], gx_count, own_rows, slab_width)
        return lax.all_to_all(pieces, "gx", 1, 1, tiled=True)

    position = lax.axis_index("gx")
    eigen = lax.dynamic_slice(wall_eigen, (position * own_rows,), (own_rows,))
    mode = jnp.arange(half, dtype=jnp.int32)
    damping = damping_of(diffusivity, eigen, mode, total)
    last = damping_of(diffusivity, eigen, jnp.full((1,), half, jnp.int32), total)
    travel = 2.0 * math.pi / total * mode.astype(jnp.float32) * bulk_shift[0]
    last_cos = jnp.cos(-math.pi * bulk_shift[0])

    def filter_rows(values, first):
        count = values.shape[0]
        damp = damping[first : first + count]
        end = last[first : first + count]
        if total <= DENSE_LIMIT:
            table = jnp.asarray(real_table(total)).reshape(gx_count, slab_width, total)
            spec = jnp.einsum("fsaj,sjk->fak", values, table, precision=lax.Precision.HIGH)
            real, imag = spec[..., :half], spec[..., half:]
            weight = jnp.where(mode == 0, 1.0, 2.0) / total
            cosine = damp * (weight * jnp.cos(travel))
            sine = damp * (weight * jnp.sin(travel))
            turned = jnp.where(mode == 0, end * (last_cos / total), cosine)
            spec = jnp.concatenate(
                [real * cosine + imag * sine, imag * turned - real * sine], axis=-1
            )
            return jnp.einsum("fak,sjk->fsaj", spec, table, precision=lax.Precision.HIGH)
        flat = values.transpose(0, 2, 1, 3).reshape(count, own_rows, total)
        spec = jnp.fft.rfft(flat, axis=-1)
        full = jnp.concatenate([damp, end], axis=-1)
        angle = jnp.append(travel, -math.pi * bulk_shift[0])
        spec = spec * lax.complex(full * jnp.cos(angle), -full * jnp.sin(angle))
        back = jnp.fft.irfft(spec, n=total, axis=-1)
        return back.reshape(count, own_rows, gx_count, slab_width).transpose(0, 2, 1, 3)

    parts = []
    for first, group in ((0, field[:2]), (2, field[2:] + source)):
        rows = scatter_rows(project(dual_part, group))
        back = scatter_rows(filter_rows(rows, first))
        filtered = back.reshape(group.shape)
        parts.append(project(basis_part, filtered))
    return jnp.concatenate(parts)[:, None]


def solution(mesh):
    in_specs = (
        P(None, "gz", None, "gx"),
        P(("gx", "gz")),
        P(("gx", "gz")),
        P(None, ("gx", "gz")),
        P(),
        P(),
        P(),
        P(),
        P(),
    )
    out_specs = P(None, "gz", None, "gx")
    return jax.shard_map(
        per_device, mesh=mesh, in_specs=in_specs, out_specs=out_specs, check_vma=False
    )
```

time: 466 us -> 122 us (0.26)
  the two profiles are of different devices: /device:TPU:13 before, /device:TPU:0 now
where the time goes in v1:
time: 122 us; the launch traced here: 121 us
  waiting for transfers between devices  41.7 us (34%)
  matrix products  21.4 us (18%)
  starting transfers between devices  17.3 us (14%)
  local copies, waits for them, and re-layouts  16 us (13%)
  Pallas kernels  10.4 us (9%)
  blocking collectives  7.19 us (6%)
  other arithmetic  5.97 us (5%)
    all_to_all x4, waiting for transfers between devices, scatter_rows(): return lax.all_to_all(pieces, 'gx', 1, 1, tiled=True)  41.7 us
    all_to_all x4, starting transfers between devices, scatter_rows(): return lax.all_to_all(pieces, 'gx', 1, 1, tiled=True)  17.3 us
    pallas_call x1, Pallas kernels, deposit(): pl.pallas_call(functools.partial(deposit_kernel, slab_width), grid=(drops...  10.4 us
    dot_general x4, matrix products, project(): jnp.einsum('ay,fyx->fax', matrix, values, precision=lax.Precision.HIGH)  7.44 us
    dot_general x2, matrix products, filter_rows(): jnp.einsum('fsaj,sjk->fak', values, table, precision=lax.Precision.HIGH)  7.24 us
    all_gather x1, blocking collectives, per_device(): drops = lax.all_gather(drops, 'gz', axis=1, tiled=True)  7.19 us
    dot_general x2, matrix products, filter_rows(): jnp.einsum('fak,sjk->fsaj', spec, table, precision=lax.Precision.HIGH)  6.71 us
    unnamed x12, local copies, waits for them, and re-layouts  2.59 us
  transfers between devices with their start and end apart: 4, of which 4 were waited for; matrix products, arithmetic and copies ran while one was open for 13% of the time, Pallas kernels for 0%

profile of v1, /device:TPU:0, one launch (start us, length us, event | category | flops | bytes accessed | tf_op | source)
XLA Modules:
  0.0 121.0 jit_solution(1198800092699385138)
XLA Ops:
  0.0 0.0 copy-start
  0.0 0.8 convert_element_type.32
  0.8 0.7 convert_element_type.33
  1.5 0.8 pad_maximum_fusion
  2.3 7.2 %all_gather.3 = f32[4,16384]{1,0:T(4,128)S(1)} all-gather(f32[4,4096]{1,0:T(4,128)S(1)} %pad_maximum_fusion), channel_id=1, replica_groups=mesh['gx'=8,'gz'=4] {'gz'}, dimensions={1}, use_global_device_ids=true | all-gather | bytes 327680 | tf_op jit(solution)/shard_map/all_gather | solution.py:90
  9.5 0.2 and_select_fusion
  9.8 0.1 slice.65.rate_ref
  9.8 0.4 compare_select_fusion.row_ref
  10.2 10.4 %shard_map.109 = f32[512,512]{1,0:T(8,128)S(1)} custom-call(s32[1,16384]{1,0:T(1,128)S(1)} %compare_select_fusion.row_ref, s32[1,16384]{1,0:T(1,128)S(1)} %get-tuple-element.7.col_ref, f32[2,16384]{1,0:T(2,128)S(1)} %slice.65.rate_ref), custom_call_target="tpu_custom_call" | custom-call | tf_op jit(solution)/shard_map/pallas_call | solution.py:50
  20.7 0.7 reshape.145
  21.3 1.6 %reduce_sum.9 = f32[512,2,128]{2,1,0:T(2,128)S(1)} reduce(f32[512,2,2,128]{3,2,1,0:T(2,128)S(1)} %reshape.145, f32[]{:T(128)} %constant.69.clone.1), dimensions={2}, to_apply=%region_0.1 | reduce | flops 131072 | bytes 1572868 | tf_op jit(solution)/shard_map/reduce_sum | solution.py:62
  23.0 0.2 copy.53
  23.2 2.2 %fusion.19 = (f32[2,1,512,128]{3,2,1,0:T(8,128)}, f32[2,1,512,128]{3,2,1,0:T(8,128)}) fusion(f32[4,1,512,128]{3,2,1,0:T(8,128)} %param.11), kind=kLoop, calls=%fused_computation.62 | loop fusion | bytes 2097152 | tf_op jit(solution)/shard_map/slice | solution.py:137
  25.4 0.0 copy-start.3
  25.4 1.3 %copy.67 = f32[2,1,512,128]{2,3,0,1:T(8,128)S(1)} copy(f32[2,1,512,128]{3,2,1,0:T(8,128)} %get-tuple-element.14) | data formatting | bytes 1048576
  26.8 0.0 copy-done
  26.8 1.4 %fusion.1 = f32[2,512,128]{1,2,0:T(8,128)} fusion(f32[512,512]{1,0:T(8,128)S(1)} %copy-done, f32[512,2,128]{0,2,1:T(8,128)S(1)} %copy.53, f32[2,1,512,128]{2,3,0,1:T(8,128)S(1)} %copy.67), kind=kOutput, calls=%fused_computation.3 | convolution fusion | flops 403046400 | bytes 2621440 | tf_op jit(solution)/shard_map/ay,fyx->fax/dot_general | solution.py:98
  28.2 1.2 %copy.54 = f32[2,512,128]{2,1,0:T(8,128)S(1)} copy(f32[2,512,128]{1,2,0:T(8,128)} %fusion.1) | data formatting | bytes 1048576 | tf_op jit(solution)/shard_map/add | solution.py:98
  29.4 0.0 copy-start.4
  29.4 0.8 copy.55
  30.3 5.9 %all-to-all-start.2 = ((f32[2,8,64,128]{3,2,0,1:T(8,128)}), f32[2,8,64,128]{3,2,0,1:T(8,128)S(1)}, u32[]{:S(2)}, u32[]{:S(2)}) async-start(f32[2,8,64,128]{3,2,0,1:T(8,128)} %copy.55), calls=%async_computation.2 | async-start | bytes 1048576 | tf_op jit(solution)/shard_map/all_to_all | solution.py:102
  36.9 1.2 %copy.66 = f32[2,1,512,128]{2,3,0,1:T(8,128)S(1)} copy(f32[2,1,512,128]{3,2,1,0:T(8,128)} %get-tuple-element.13) | data formatting | bytes 1048576
  38.1 0.0 copy-done.3
  38.1 1.8 %fusion.3 = f32[2,512,128]{1,2,0:T(8,128)} fusion(f32[512,512]{1,0:T(8,128)S(1)} %copy-done, f32[2,1,512,128]{2,3,0,1:T(8,128)S(1)} %copy.66, f32[4,1,512,128]{3,2,1,0:T(8,128)S(1)} %copy-done.3), kind=kOutput, calls=%fused_computation.7 | convolution fusion | flops 402784256 | bytes 2621440 | tf_op jit(solution)/shard_map/ay,fyx->fax/dot_general | solution.py:98
  40.0 1.2 %copy.46 = f32[2,512,128]{2,1,0:T(8,128)S(1)} copy(f32[2,512,128]{1,2,0:T(8,128)} %fusion.3) | data formatting | bytes 1048576 | tf_op jit(solution)/shard_map/add | solution.py:98
  41.2 0.8 copy.47
  42.1 0.8 broadcast_add_fusion.1
  42.8 0.0 copy-done.4
  42.8 0.1 fusion.15
  42.9 8.2 %all-to-all-done.2 = f32[2,8,64,128]{3,2,0,1:T(8,128)S(1)} async-done(((f32[2,8,64,128]{3,2,0,1:T(8,128)}), f32[2,8,64,128]{3,2,0,1:T(8,128)S(1)}, u32[]{:S(2)}, u32[]{:S(2)}) %all-to-all-start.2) | async-done | bytes 524320 | tf_op jit(solution)/shard_map/all_to_all | solution.py:102
  51.2 3.7 %all-to-all-start = ((f32[2,8,64,128]{3,2,0,1:T(8,128)}), f32[2,8,64,128]{3,2,0,1:T(8,128)S(1)}, u32[]{:S(2)}, u32[]{:S(2)}) async-start(f32[2,8,64,128]{3,2,0,1:T(8,128)} %copy.47), calls=%async_computation | async-start | bytes 1048576 | tf_op jit(solution)/shard_map/all_to_all | solution.py:102
  54.9 0.1 broadcast_add_fusion
  55.0 0.2 fusion.8
  55.1 3.5 %convolution_bitcast_fusion.5 = f32[2,64,1024]{2,1,0:T(8,128)S(1)} fusion(f32[2,8,64,128]{3,2,0,1:T(8,128)S(1)} %all-to-all-done.2, f32[8,128,1024,1]{2,1,3,0:T(8,128)} %constant.73), kind=kOutput, calls=%fused_computation.9 | convolution fusion | flops 805306368 | bytes 5242880 | tf_op jit(solution)/shard_map/fsaj,sjk->fak/dot_general | solution.py:118
  58.7 10.8 %all-to-all-done = f32[2,8,64,128]{3,2,0,1:T(8,128)S(1)} async-done(((f32[2,8,64,128]{3,2,0,1:T(8,128)}), f32[2,8,64,128]{3,2,0,1:T(8,128)S(1)}, u32[]{:S(2)}, u32[]{:S(2)}) %all-to-all-start) | async-done | bytes 524320 | tf_op jit(solution)/shard_map/all_to_all | solution.py:102
  69.5 0.0 copy-start.1
  69.5 3.7 %convolution_bitcast_fusion.7 = f32[2,64,1024]{2,1,0:T(8,128)S(1)} fusion(f32[2,8,64,128]{3,2,0,1:T(8,128)S(1)} %all-to-all-done, f32[8,128,1024,1]{2,1,3,0:T(8,128)} %constant.73), kind=kOutput, calls=%fused_computation.11 | convolution fusion | flops 805306368 | bytes 5242880 | tf_op jit(solution)/shard_map/fsaj,sjk->fak/dot_general | solution.py:118
  73.2 0.2 multiply_add_fusion.1
  73.4 0.0 copy-done.1
  73.4 2.3 %convolution_bitcast_fusion.6 = f32[2,8,64,128]{3,2,1,0:T(8,128)S(1)} fusion(f32[8,128,1024,1]{2,1,0,3:T(8,128)S(1)} %copy-done.1, f32[2,64,512]{2,1,0:T(8,128)S(1)} %get-tuple-element.15, f32[2,64,512]{2,1,0:T(8,128)S(1)} %get-tuple-element.16), kind=kOutput, calls=%fused_computation.10 | convolution fusion | flops 805437440 | bytes 5242880 | tf_op jit(solution)/shard_map/fak,sjk->fsaj/dot_general | solution.py:127
  75.7 0.8 copy.48
  76.6 3.6 %all-to-all-start.1 = ((f32[2,8,64,128]{3,2,0,1:T(8,128)}), f32[2,8,64,128]{3,2,0,1:T(8,128)S(1)}, u32[]{:S(2)}, u32[]{:S(2)}) async-start(f32[2,8,64,128]{3,2,0,1:T(8,128)} %copy.48), calls=%async_computation.1 | async-start | bytes 1048576 | tf_op jit(solution)/shard_map/all_to_all | solution.py:102
  80.2 4.4 %convolution_bitcast_fusion.4 = f32[2,8,64,128]{3,2,1,0:T(8,128)S(1)} fusion(f32[8,128,1024,1]{2,1,0,3:T(8,128)} %constant.74, f32[2,64,512]{2,1,0:T(8,128)S(1)} %get-tuple-element.12, f32[2,64,512]{2,1,0:T(8,128)S(1)} %get-tuple-element.11), kind=kOutput, calls=%fused_computation.8 | convolution fusion | flops 805437440 | bytes 5242880 | tf_op jit(solution)/shard_map/fak,sjk->fsaj/dot_general | solution.py:127
  84.6 0.0 copy-start.2
  84.6 0.8 copy.56
  85.4 9.4 %all-to-all-done.1 = f32[2,8,64,128]{3,2,0,1:T(8,128)S(1)} async-done(((f32[2,8,64,128]{3,2,0,1:T(8,128)}), f32[2,8,64,128]{3,2,0,1:T(8,128)S(1)}, u32[]{:S(2)}, u32[]{:S(2)}) %all-to-all-start.1) | async-done | bytes 524320 | tf_op jit(solution)/shard_map/all_to_all | solution.py:102
  94.9 4.1 %all-to-all-start.3 = ((f32[2,8,64,128]{3,2,0,1:T(8,128)}), f32[2,8,64,128]{3,2,0,1:T(8,128)}, u32[]{:S(2)}, u32[]{:S(2)}) async-start(f32[2,8,64,128]{3,2,0,1:T(8,128)} %copy.56), calls=%async_computation.3 | async-start | bytes 1048576 | tf_op jit(solution)/shard_map/all_to_all | solution.py:102
  99.1 1.0 copy.51
  100.1 13.2 %all-to-all-done.3 = f32[2,8,64,128]{3,2,0,1:T(8,128)} async-done(((f32[2,8,64,128]{3,2,0,1:T(8,128)}), f32[2,8,64,128]{3,2,0,1:T(8,128)}, u32[]{:S(2)}, u32[]{:S(2)}) %all-to-all-start.3) | async-done | bytes 524320 | tf_op jit(solution)/shard_map/all_to_all | solution.py:102
  113.3 1.1 copy.57
  114.4 1.0 copy.59
  115.4 0.0 copy-done.2
  115.4 2.1 %fusion.2 = f32[2,512,128]{1,2,0:T(8,128)S(1)} fusion(f32[2,512,128]{1,2,0:T(8,128)} %copy.51, f32[2,512,128]{2,1,0:T(8,128)S(1)} %bitcast.86, f32[512,512]{1,0:T(8,128)S(1)} %copy-done.2), kind=kOutput, calls=%fused_computation.5 | convolution fusion | flops 402784256 | bytes 2621440 | tf_op jit(solution)/shard_map/ay,fyx->fax/dot_general | solution.py:98
  117.5 2.1 %fusion = f32[2,512,128]{1,2,0:T(8,128)S(1)} fusion(f32[2,512,128]{1,2,0:T(8,128)} %copy.59, f32[2,512,128]{2,1,0:T(8,128)S(1)} %bitcast.88, f32[512,512]{1,0:T(8,128)S(1)} %copy-done.2), kind=kOutput, calls=%fused_computation.1 | convolution fusion | flops 402784256 | bytes 2621440 | tf_op jit(solution)/shard_map/ay,fyx->fax/dot_general | solution.py:98
  119.6 0.1 maximum_bitcast_fusion
  119.7 1.3 %copy.60 = f32[4,1,512,128]{3,2,1,0:T(8,128)} copy(f32[4,1,512,128]{2,3,0,1:T(8,128)S(1)} %maximum_bitcast_fusion) | data formatting | bytes 2097152 | tf_op jit(solution)/shard_map/broadcast_in_dim | solution.py:142
  (5 shorter events, 0.1 us)
Async XLA Ops:
  0.0 26.8 %copy-start = (f32[512,512]{1,0:T(8,128)S(1)}, f32[512,512]{1,0:T(8,128)}, u32[]{:S(2)}) copy-start(f32[512,512]{1,0:T(8,128)} %param.18) | copy-start | bytes 3145732
  25.4 12.7 %copy-start.3 = (f32[4,1,512,128]{3,2,1,0:T(8,128)S(1)}, f32[4,1,512,128]{3,2,1,0:T(8,128)}, u32[]{:S(2)}) copy-start(f32[4,1,512,128]{3,2,1,0:T(8,128)} %param.11) | copy-start | bytes 3145732
  29.4 13.4 %copy-start.4 = (f32[4]{0:T(128)S(1)}, f32[4]{0:T(128)}, u32[]{:S(2)}) copy-start(f32[4]{0:T(128)} %param.15) | copy-start | bytes 52
  30.3 20.9 %all-to-all-start.2 = ((f32[2,8,64,128]{3,2,0,1:T(8,128)}), f32[2,8,64,128]{3,2,0,1:T(8,128)S(1)}, u32[]{:S(2)}, u32[]{:S(2)}) async-start(f32[2,8,64,128]{3,2,0,1:T(8,128)} %copy.55), calls=%async_computation.2 | async-start | bytes 1048576 | tf_op jit(solution)/shard_map/all_to_all | solution.py:102
  51.2 18.3 %all-to-all-start = ((f32[2,8,64,128]{3,2,0,1:T(8,128)}), f32[2,8,64,128]{3,2,0,1:T(8,128)S(1)}, u32[]{:S(2)}, u32[]{:S(2)}) async-start(f32[2,8,64,128]{3,2,0,1:T(8,128)} %copy.47), calls=%async_computation | async-start | bytes 1048576 | tf_op jit(solution)/shard_map/all_to_all | solution.py:102
  69.5 3.9 %copy-start.1 = (f32[8,128,1024,1]{2,1,0,3:T(8,128)S(1)}, f32[8,128,1024,1]{2,1,0,3:T(8,128)}, u32[]{:S(2)}) copy-start(f32[8,128,1024,1]{2,1,0,3:T(8,128)} %constant.74) | copy-start | bytes 12582916
  76.6 18.3 %all-to-all-start.1 = ((f32[2,8,64,128]{3,2,0,1:T(8,128)}), f32[2,8,64,128]{3,2,0,1:T(8,128)S(1)}, u32[]{:S(2)}, u32[]{:S(2)}) async-start(f32[2,8,64,128]{3,2,0,1:T(8,128)} %copy.48), calls=%async_computation.1 | async-start | bytes 1048576 | tf_op jit(solution)/shard_map/all_to_all | solution.py:102
  84.6 30.8 %copy-start.2 = (f32[512,512]{1,0:T(8,128)S(1)}, f32[512,512]{1,0:T(8,128)}, u32[]{:S(2)}) copy-start(f32[512,512]{1,0:T(8,128)} %param.17) | copy-start | bytes 3145732
  94.9 18.5 %all-to-all-start.3 = ((f32[2,8,64,128]{3,2,0,1:T(8,128)}), f32[2,8,64,128]{3,2,0,1:T(8,128)}, u32[]{:S(2)}, u32[]{:S(2)}) async-start(f32[2,8,64,128]{3,2,0,1:T(8,128)} %copy.56), calls=%async_computation.3 | async-start | bytes 1048576 | tf_op jit(solution)/shard_map/all_to_all | solution.py:102

commit v2 on v1

--- a/solution.py
+++ b/solution.py
@@ -9,7 +9,7 @@
 from jax.experimental.pallas import tpu as pltpu
 from jax.sharding import PartitionSpec as P
 
-DENSE_LIMIT = 2048
+DENSE_PARTS = 16
 
 
 def real_table(total):
@@ -19,6 +19,299 @@
     sines = -np.sin(angle)
     sines[:, 0] = 1.0 - 2.0 * (np.arange(total) % 2)
     return np.concatenate([np.cos(angle), sines], axis=1).astype(np.float32)
+
+
+def split_two(values):
+    high = values.astype(jnp.bfloat16)
+    return high, (values - high.astype(jnp.float32)).astype(jnp.bfloat16)
+
+
+def product(left, right, transposed=False):
+    return lax.dot_general(
+        left,
+        right,
+        (((1,), (1 if transposed else 0,)), ((), ())),
+        preferred_element_type=jnp.float32,
+    )
+
+
+def step_kernel(
+    gx_count,
+    gz_count,
+    field_ref,
+    drop_ref,
+    dual_ref,
+    basis_ref,
+    eigen_ref,
+    aux_ref,
+    high_hbm,
+    low_hbm,
+    out_ref,
+    high_ref,
+    low_ref,
+    matrix_ref,
+    gathered,
+    total_ref,
+    send_one,
+    recv_one,
+    send_two,
+    recv_two,
+    drop_send,
+    drop_recv,
+    one_send,
+    one_recv,
+    two_send,
+    two_recv,
+    load_sem,
+):
+    field_count, row_count, slab_width = field_ref.shape
+    own_rows = row_count // gx_count
+    pairs = field_count // 2
+    half = gx_count * slab_width // 2
+    me = lax.axis_index("gx")
+    plane = lax.axis_index("gz")
+
+    barrier = pltpu.get_barrier_semaphore()
+    for off in range(1, gx_count):
+        pl.semaphore_signal(
+            barrier,
+            inc=1,
+            device_id=(lax.rem(me + off, gx_count), plane),
+            device_id_type=pl.DeviceIdType.MESH,
+        )
+    for off in range(1, gz_count):
+        pl.semaphore_signal(
+            barrier,
+            inc=1,
+            device_id=(me, lax.rem(plane + off, gz_count)),
+            device_id_type=pl.DeviceIdType.MESH,
+        )
+    pl.semaphore_wait(barrier, gx_count + gz_count - 2)
+
+    drop_copies = []
+    for off in range(1, gz_count):
+        copy = pltpu.make_async_remote_copy(
+            src_ref=drop_ref,
+            dst_ref=gathered.at[off],
+            send_sem=drop_send.at[off],
+            recv_sem=drop_recv.at[off],
+            device_id=(me, lax.rem(plane + off, gz_count)),
+            device_id_type=pl.DeviceIdType.MESH,
+        )
+        copy.start()
+        drop_copies.append(copy)
+    loads = [
+        pltpu.make_async_copy(high_hbm, high_ref, load_sem.at[0]),
+        pltpu.make_async_copy(low_hbm, low_ref, load_sem.at[1]),
+    ]
+    for copy in loads:
+        copy.start()
+
+    def load_matrix(ref):
+        high, low = split_two(ref[...])
+        matrix_ref[:, :row_count] = high
+        matrix_ref[:, row_count : 2 * row_count] = low
+        matrix_ref[:, 2 * row_count :] = high
+
+    def apply_matrix(values):
+        high, low = split_two(values)
+        return values + product(matrix_ref[...], jnp.concatenate([high, high, low], axis=0))
+
+    def exchange(pair, source, landing, send_sem, recv_sem):
+        copies = []
+        for off in range(1, gx_count):
+            target = lax.rem(me + off, gx_count)
+            copy = pltpu.make_async_remote_copy(
+                src_ref=source.at[pl.ds(2 * pair, 2), target],
+                dst_ref=landing.at[pl.ds(2 * pair, 2), me],
+                send_sem=send_sem.at[pair * gx_count + off],
+                recv_sem=recv_sem.at[pair * gx_count + off],
+                device_id=(target, plane),
+                device_id_type=pl.DeviceIdType.MESH,
+            )
+            copy.start()
+            copies.append(copy)
+        landing[pl.ds(2 * pair, 2), me] = source[pl.ds(2 * pair, 2), me]
+        return copies
+
+    def project(pair, values):
+        values = apply_matrix(values)
+        for side in range(2):
+            send_one[2 * pair + side] = values[
+                :, side * slab_width : (side + 1) * slab_width
+            ].reshape(gx_count, own_rows, slab_width)
+        return exchange(pair, send_one, recv_one, one_send, one_recv)
+
+    load_matrix(dual_ref)
+    first = [project(0, jnp.concatenate([field_ref[0], field_ref[1]], axis=1))]
+
+    gathered[0] = drop_ref[...]
+    total_ref[...] = jnp.zeros_like(total_ref)
+    for copy in drop_copies:
+        copy.wait()
+    drops = drop_ref.shape[1]
+    block = min(2048, drops)
+    blocks = drops // block
+
+    def deposit(step, carry):
+        packet = gathered[step // blocks, :, pl.ds(pl.multiple_of(step % blocks * block, 128), block)]
+        cell = packet[0:1].astype(jnp.int32)
+        mine = packet[1:2].astype(jnp.int32) == plane
+        row = jnp.where(mine, cell // slab_width, -1)
+        col = cell % slab_width
+        hit = lax.broadcasted_iota(jnp.int32, (row_count, block), 0) == row
+        left = jnp.where(hit, 1.0, 0.0).astype(jnp.bfloat16)
+        here = lax.broadcasted_iota(jnp.int32, (slab_width, block), 0) == col
+        terms = []
+        for component in range(2):
+            rate = packet[2 + component : 3 + component]
+            high = rate.astype(jnp.bfloat16).astype(jnp.float32)
+            for part in (high, rate - high):
+                terms.append(jnp.where(here, part, 0.0).astype(jnp.bfloat16))
+        total_ref[...] += product(left, jnp.concatenate(terms, axis=0), transposed=True)
+        return carry
+
+    lax.fori_loop(0, gz_count * blocks, deposit, 0)
+    merged = []
+    for component in range(2):
+        base = 2 * component * slab_width
+        merged.append(
+            field_ref[2 + component]
+            + total_ref[:, base : base + slab_width]
+            + total_ref[:, base + slab_width : base + 2 * slab_width]
+        )
+    first.append(project(1, jnp.concatenate(merged, axis=1)))
+    load_matrix(basis_ref)
+
+    for copy in loads:
+        copy.wait()
+    eigen = eigen_ref[pl.ds(pl.multiple_of(me * own_rows, 8), own_rows), :]
+    second = []
+    for pair in range(pairs):
+        damps = []
+        for which in range(2):
+            growth = jnp.concatenate(
+                [
+                    aux_ref[5 + 2 * pair + side : 6 + 2 * pair + side, :]
+                    * (eigen + aux_ref[which : which + 1, :])
+                    for side in range(2)
+                ],
+                axis=0,
+            )
+            damps.append((1.0 - growth) / (1.0 + growth))
+        cosine = damps[0] * aux_ref[2:3, :]
+        sine = damps[0] * aux_ref[3:4, :]
+        turned = damps[1] * aux_ref[4:5, :]
+        for copy in first[pair]:
+            copy.wait()
+        rows = jnp.concatenate(
+            [
+                recv_one[2 * pair : 2 * pair + 2, slab].reshape(2 * own_rows, slab_width)
+                for slab in range(gx_count)
+            ],
+            axis=1,
+        )
+        high, low = split_two(rows)
+        spec = product(high, high_ref[...]) + product(low, high_ref[...])
+        spec += product(high, low_ref[...])
+        real, imag = spec[:, :half], spec[:, half:]
+        spec = jnp.concatenate([real * cosine + imag * sine, imag * turned - real * sine], axis=1)
+        high, low = split_two(spec)
+        back = product(high, high_ref[...], True) + product(low, high_ref[...], True)
+        back += product(high, low_ref[...], True)
+        for slab in range(gx_count):
+            send_two[2 * pair : 2 * pair + 2, slab] = back[
+                :, slab * slab_width : (slab + 1) * slab_width
+            ].reshape(2, own_rows, slab_width)
+        second.append(exchange(pair, send_two, recv_two, two_send, two_recv))
+    for pair in range(pairs):
+        for copy in second[pair]:
+            copy.wait()
+        values = apply_matrix(
+            jnp.concatenate(
+                [recv_two[2 * pair + side].reshape(row_count, slab_width) for side in range(2)],
+                axis=1,
+            )
+        )
+        for side in range(2):
+            out_ref[2 * pair + side] = values[:, side * slab_width : (side + 1) * slab_width]
+
+
+def dense_step(
+    field, drop_cell, drop_plane, drop_rate, diffusivity, wall_eigen, basis_part, dual_part, bulk_shift
+):
+    field_count, _, row_count, slab_width = field.shape
+    gx_count = lax.axis_size("gx")
+    gz_count = lax.axis_size("gz")
+    total = slab_width * gx_count
+    half = total // 2
+    own_rows = row_count // gx_count
+    drops = jnp.concatenate(
+        [
+            drop_cell.astype(jnp.float32)[None],
+            drop_plane.astype(jnp.float32)[None],
+            drop_rate,
+        ]
+    )
+    mode = np.arange(half)
+    wave = (2.0 * np.pi / total * mode).astype(np.float32)
+    square = wave * wave
+    ends = np.where(mode == 0, np.float32(np.pi) ** 2, square).astype(np.float32)
+    weight = (np.where(mode == 0, 1.0, 2.0) / total).astype(np.float32)
+    travel = jnp.asarray(wave) * bulk_shift[0]
+    cosine = jnp.asarray(weight) * jnp.cos(travel)
+    sine = jnp.asarray(weight) * jnp.sin(travel)
+    turned = jnp.where(jnp.asarray(mode == 0), jnp.cos(-math.pi * bulk_shift[0]) / total, cosine)
+    aux = jnp.concatenate(
+        [
+            jnp.stack([jnp.asarray(square), jnp.asarray(ends), cosine, sine, turned]),
+            jnp.broadcast_to(diffusivity[:, None], (field_count, half)),
+        ]
+    )
+    table = real_table(total)
+    high = table.astype(jnp.bfloat16)
+    low = (table - high.astype(np.float32)).astype(jnp.bfloat16)
+    piece = (field_count, gx_count, own_rows, slab_width)
+    vmem = pl.BlockSpec(memory_space=pltpu.VMEM)
+    hbm = pl.BlockSpec(memory_space=pl.ANY)
+    links = field_count // 2 * gx_count
+    out = pl.pallas_call(
+        functools.partial(step_kernel, gx_count, gz_count),
+        out_shape=jax.ShapeDtypeStruct((field_count, row_count, slab_width), jnp.float32),
+        in_specs=[vmem] * 6 + [hbm] * 2,
+        out_specs=vmem,
+        scratch_shapes=[
+            pltpu.VMEM((total, total), jnp.bfloat16),
+            pltpu.VMEM((total, total), jnp.bfloat16),
+            pltpu.VMEM((row_count, 3 * row_count), jnp.bfloat16),
+            pltpu.VMEM((gz_count,) + drops.shape, jnp.float32),
+            pltpu.VMEM((row_count, 4 * slab_width), jnp.float32),
+            pltpu.VMEM(piece, jnp.float32),
+            pltpu.VMEM(piece, jnp.float32),
+            pltpu.VMEM(piece, jnp.float32),
+            pltpu.VMEM(piece, jnp.float32),
+            pltpu.SemaphoreType.DMA((gz_count,)),
+            pltpu.SemaphoreType.DMA((gz_count,)),
+            pltpu.SemaphoreType.DMA((links,)),
+            pltpu.SemaphoreType.DMA((links,)),
+            pltpu.SemaphoreType.DMA((links,)),
+            pltpu.SemaphoreType.DMA((links,)),
+            pltpu.SemaphoreType.DMA((2,)),
+        ],
+        compiler_params=pltpu.CompilerParams(
+            collective_id=0, has_side_effects=True, vmem_limit_bytes=48 * 2**20
+        ),
+    )(
+        field.reshape(field_count, row_count, slab_width),
+        drops,
+        dual_part,
+        basis_part,
+        wall_eigen[:, None],
+        aux,
+        jnp.asarray(high),
+        jnp.asarray(low),
+    )
+    return out[:, None]
 
 
 def deposit_kernel(slab_width, row_ref, col_ref, rate_ref, out_ref):
@@ -107,24 +400,11 @@
     damping = damping_of(diffusivity, eigen, mode, total)
     last = damping_of(diffusivity, eigen, jnp.full((1,), half, jnp.int32), total)
     travel = 2.0 * math.pi / total * mode.astype(jnp.float32) * bulk_shift[0]
-    last_cos = jnp.cos(-math.pi * bulk_shift[0])
 
     def filter_rows(values, first):
         count = values.shape[0]
         damp = damping[first : first + count]
         end = last[first : first + count]
-        if total <= DENSE_LIMIT:
-            table = jnp.asarray(real_table(total)).reshape(gx_count, slab_width, total)
-            spec = jnp.einsum("fsaj,sjk->fak", values, table, precision=lax.Precision.HIGH)
-            real, imag = spec[..., :half], spec[..., half:]
-            weight = jnp.where(mode == 0, 1.0, 2.0) / total
-            cosine = damp * (weight * jnp.cos(travel))
-            sine = damp * (weight * jnp.sin(travel))
-            turned = jnp.where(mode == 0, end * (last_cos / total), cosine)
-            spec = jnp.concatenate(
-                [real * cosine + imag * sine, imag * turned - real * sine], axis=-1
-            )
-            return jnp.einsum("fak,sjk->fsaj", spec, table, precision=lax.Precision.HIGH)
         flat = values.transpose(0, 2, 1, 3).reshape(count, own_rows, total)
         spec = jnp.fft.rfft(flat, axis=-1)
         full = jnp.concatenate([damp, end], axis=-1)
@@ -155,6 +435,7 @@
         P(),
     )
     out_specs = P(None, "gz", None, "gx")
+    body = dense_step if mesh.shape["gx"] <= DENSE_PARTS else per_device
     return jax.shard_map(
-        per_device, mesh=mesh, in_specs=in_specs, out_specs=out_specs, check_vma=False
-    )
+        body, mesh=mesh, in_specs=in_specs, out_specs=out_specs, check_vma=False
+    )

time: 122 us -> 67.6 us (0.55)
  the two profiles are of different devices: /device:TPU:0 before, /device:TPU:13 now
where the time goes in v2:
time: 67.6 us; the launch traced here: 67.1 us
  Pallas kernels  56.3 us (83%)
  local copies, waits for them, and re-layouts  7.01 us (10%)
  other arithmetic  3.01 us (4%)
  between operations  0.77 us (1%)
    pallas_call x1, Pallas kernels, dense_step(): pl.pallas_call(functools.partial(step_kernel, gx_count, gz_count), out_sh...  56.3 us
    unnamed x7, local copies, waits for them, and re-layouts  4.64 us

profile of v2, /device:TPU:13, one launch (start us, length us, event | category | flops | bytes accessed | tf_op | source)
XLA Modules:
  0.0 67.1 jit_solution(6683569635650935507)
XLA Ops:
  0.7 0.8 %broadcast_select_fusion = (f32[512]{0:T(512)S(1)}, f32[512]{0:T(512)S(1)}, f32[512]{0:T(512)S(1)}) fusion(pred[512]{0:T(512)(128)(4,1)} %constant.21.clone, f32[]{:T(128)S(6)} %div.3, f32[512]{0:T(512)} %constant.20.clone, f32[512]{0:T(512)} %constant.19.clone, f32[]{:T(128)} %bitcast.11), kind=kLoop, calls=%fused_computation.5 | loop fusion | flops 2048 | bytes 10760 | tf_op jit(solution)/shard_map/jit(_where)/select_n | solution.py:264
  1.5 0.7 %broadcast_in_dim.26 = f32[4,512]{1,0:T(4,128)S(1)} broadcast(f32[4]{0:T(128)} %param.20), dimensions={0} | broadcast | bytes 8208 | tf_op jit(solution)/shard_map/broadcast_in_dim | solution.py:268
  2.2 0.7 %convert_element_type.6 = f32[4096]{0:T(1024)S(1)} convert(s32[4096]{0:T(1024)} %param.17) | non-fusion elementwise | flops 4096 | bytes 32768 | tf_op jit(solution)/shard_map/convert_element_type | solution.py:251
  2.9 0.7 %convert_element_type.7 = f32[4096]{0:T(1024)S(1)} convert(s32[4096]{0:T(1024)} %param.18) | non-fusion elementwise | flops 4096 | bytes 32768 | tf_op jit(solution)/shard_map/convert_element_type | solution.py:252
  3.7 0.8 %concatenate.7.aux_ref = f32[9,512]{1,0:T(8,128)S(1)} concatenate(f32[1,512]{1,0:T(1,128)} %constant.27, f32[1,512]{1,0:T(1,128)} %constant.28, f32[1,512]{1,0:T(1,128)S(1)} %bitcast.19, f32[1,512]{1,0:T(1,128)S(1)} %bitcast.18, f32[1,512]{1,0:T(1,128)S(1)} %bitcast.17, f32[4,512]{1,0:T(4,128)S(1)} %broadcast_in_dim.26), dimensions={0} | concatenate | bytes 36864 | tf_op jit(solution)/shard_map/concatenate | solution.py:265
  4.5 0.8 %pad_maximum_fusion.drop_ref = f32[4,4096]{1,0:T(4,128)S(1)} fusion(f32[2,4096]{1,0:T(2,128)} %param.19, f32[1,4096]{1,0:T(1,128)S(1)} %bitcast.16, f32[1,4096]{1,0:T(1,128)S(1)} %bitcast.15), kind=kLoop, calls=%fused_computation | loop fusion | flops 32768 | bytes 131072 | tf_op jit(solution)/shard_map/concatenate | solution.py:249
  5.3 0.8 %copy.18.eigen_ref = f32[512,1]{1,0:T(8,128)S(1)} copy(f32[512,1]{0,1:T(1,128)} %bitcast.20) | data formatting | bytes 4096 | tf_op jit(solution)/shard_map/broadcast_in_dim | solution.py:309
  6.1 0.0 copy-start
  6.1 1.2 %copy-done = f32[4,1,512,128]{3,2,1,0:T(8,128)S(1)} copy-done((f32[4,1,512,128]{3,2,1,0:T(8,128)S(1)}, f32[4,1,512,128]{3,2,1,0:T(8,128)}, u32[]{:S(2)}) %copy-start) | copy-done | bytes 1048600
  7.4 0.0 copy-start.1
  7.4 1.2 %copy-done.1 = f32[512,512]{1,0:T(8,128)S(1)} copy-done((f32[512,512]{1,0:T(8,128)S(1)}, f32[512,512]{1,0:T(8,128)}, u32[]{:S(2)}) %copy-start.1) | copy-done | bytes 1048600
  8.6 0.0 copy-start.2
  8.6 1.2 %copy-done.2 = f32[512,512]{1,0:T(8,128)S(1)} copy-done((f32[512,512]{1,0:T(8,128)S(1)}, f32[512,512]{1,0:T(8,128)}, u32[]{:S(2)}) %copy-start.2) | copy-done | bytes 1048600
  9.8 56.3 %shard_map.154 = f32[4,512,128]{2,1,0:T(8,128)S(1)} custom-call(f32[4,512,128]{2,1,0:T(8,128)S(1)} %bitcast.14, f32[4,4096]{1,0:T(4,128)S(1)} %pad_maximum_fusion.drop_ref, f32[512,512]{1,0:T(8,128)S(1)} %copy-done.1, f32[512,512]{1,0:T(8,128)S(1)} %copy-done.2, f32[512,1]{1,0:T(8,128)S(1)} %copy.18.eigen_ref, f32[9,512]{1,0:T(8,128)S(1)} %concatenate.7.aux_ref, ...), custom_call_target="tpu_custom_call" | custom-call | tf_op jit(solution)/shard_map/pallas_call | solution.py:278
  66.1 1.0 %copy.22 = f32[4,1,512,128]{3,2,1,0:T(8,128)} copy(f32[4,1,512,128]{3,2,1,0:T(8,128)S(1)} %bitcast.13) | data formatting | bytes 2097152
Async XLA Ops:
  6.1 1.2 %copy-start = (f32[4,1,512,128]{3,2,1,0:T(8,128)S(1)}, f32[4,1,512,128]{3,2,1,0:T(8,128)}, u32[]{:S(2)}) copy-start(f32[4,1,512,128]{3,2,1,0:T(8,128)} %param.16) | copy-start | bytes 3145732
  7.4 1.2 %copy-start.1 = (f32[512,512]{1,0:T(8,128)S(1)}, f32[512,512]{1,0:T(8,128)}, u32[]{:S(2)}) copy-start(f32[512,512]{1,0:T(8,128)} %dual_ref.1) | copy-start | bytes 3145732
  8.6 1.2 %copy-start.2 = (f32[512,512]{1,0:T(8,128)S(1)}, f32[512,512]{1,0:T(8,128)}, u32[]{:S(2)}) copy-start(f32[512,512]{1,0:T(8,128)} %basis_ref.1) | copy-start | bytes 3145732

commit v3 on v2

--- a/solution.py
+++ b/solution.py
@@ -38,15 +38,23 @@
 def step_kernel(
     gx_count,
     gz_count,
-    field_ref,
-    drop_ref,
-    dual_ref,
-    basis_ref,
+    cell_ref,
+    plane_ref,
+    rate_ref,
     eigen_ref,
     aux_ref,
+    diffusivity_ref,
+    shift_ref,
+    field_hbm,
+    dual_hbm,
+    basis_hbm,
     high_hbm,
     low_hbm,
     out_ref,
+    field_ref,
+    dual_ref,
+    basis_ref,
+    drop_ref,
     high_ref,
     low_ref,
     matrix_ref,
@@ -71,6 +79,15 @@
     me = lax.axis_index("gx")
     plane = lax.axis_index("gz")
 
+    loads = [
+        pltpu.make_async_copy(dual_hbm, dual_ref, load_sem.at[0]),
+        pltpu.make_async_copy(field_hbm, field_ref, load_sem.at[1]),
+        pltpu.make_async_copy(basis_hbm, basis_ref, load_sem.at[2]),
+        pltpu.make_async_copy(high_hbm, high_ref, load_sem.at[3]),
+        pltpu.make_async_copy(low_hbm, low_ref, load_sem.at[4]),
+    ]
+    for copy in loads:
+        copy.start()
     barrier = pltpu.get_barrier_semaphore()
     for off in range(1, gx_count):
         pl.semaphore_signal(
@@ -86,6 +103,9 @@
             device_id=(me, lax.rem(plane + off, gz_count)),
             device_id_type=pl.DeviceIdType.MESH,
         )
+    drop_ref[0:1] = cell_ref[...].astype(jnp.float32)
+    drop_ref[1:2] = plane_ref[...].astype(jnp.float32)
+    drop_ref[2:4] = rate_ref[...]
     pl.semaphore_wait(barrier, gx_count + gz_count - 2)
 
     drop_copies = []
@@ -100,12 +120,6 @@
         )
         copy.start()
         drop_copies.append(copy)
-    loads = [
-        pltpu.make_async_copy(high_hbm, high_ref, load_sem.at[0]),
-        pltpu.make_async_copy(low_hbm, low_ref, load_sem.at[1]),
-    ]
-    for copy in loads:
-        copy.start()
 
     def load_matrix(ref):
         high, low = split_two(ref[...])
@@ -142,7 +156,9 @@
             ].reshape(gx_count, own_rows, slab_width)
         return exchange(pair, send_one, recv_one, one_send, one_recv)
 
+    loads[0].wait()
     load_matrix(dual_ref)
+    loads[1].wait()
     first = [project(0, jnp.concatenate([field_ref[0], field_ref[1]], axis=1))]
 
     gathered[0] = drop_ref[...]
@@ -181,27 +197,34 @@
             + total_ref[:, base + slab_width : base + 2 * slab_width]
         )
     first.append(project(1, jnp.concatenate(merged, axis=1)))
+    loads[2].wait()
     load_matrix(basis_ref)
-
-    for copy in loads:
+    across = lax.broadcasted_iota(jnp.int32, (own_rows, row_count), 1)
+    down = lax.broadcasted_iota(jnp.int32, (own_rows, row_count), 0) + me * own_rows
+    eigen = jnp.sum(jnp.where(across == down, eigen_ref[...], 0.0), axis=1, keepdims=True)
+    shift = shift_ref[0]
+    weight = aux_ref[4:5, :]
+    cos_row = weight * jnp.cos(aux_ref[2:3, :] * shift)
+    sin_row = weight * jnp.sin(aux_ref[2:3, :] * shift)
+    turned_row = weight * jnp.cos(aux_ref[3:4, :] * shift)
+    for copy in loads[3:]:
         copy.wait()
-    eigen = eigen_ref[pl.ds(pl.multiple_of(me * own_rows, 8), own_rows), :]
     second = []
     for pair in range(pairs):
         damps = []
         for which in range(2):
             growth = jnp.concatenate(
                 [
-                    aux_ref[5 + 2 * pair + side : 6 + 2 * pair + side, :]
+                    diffusivity_ref[2 * pair + side]
                     * (eigen + aux_ref[which : which + 1, :])
                     for side in range(2)
                 ],
                 axis=0,
             )
             damps.append((1.0 - growth) / (1.0 + growth))
-        cosine = damps[0] * aux_ref[2:3, :]
-        sine = damps[0] * aux_ref[3:4, :]
-        turned = damps[1] * aux_ref[4:5, :]
+        cosine = damps[0] * cos_row
+        sine = damps[0] * sin_row
+        turned = damps[1] * turned_row
         for copy in first[pair]:
             copy.wait()
         rows = jnp.concatenate(
@@ -246,45 +269,37 @@
     total = slab_width * gx_count
     half = total // 2
     own_rows = row_count // gx_count
-    drops = jnp.concatenate(
-        [
-            drop_cell.astype(jnp.float32)[None],
-            drop_plane.astype(jnp.float32)[None],
-            drop_rate,
-        ]
-    )
     mode = np.arange(half)
     wave = (2.0 * np.pi / total * mode).astype(np.float32)
     square = wave * wave
     ends = np.where(mode == 0, np.float32(np.pi) ** 2, square).astype(np.float32)
     weight = (np.where(mode == 0, 1.0, 2.0) / total).astype(np.float32)
-    travel = jnp.asarray(wave) * bulk_shift[0]
-    cosine = jnp.asarray(weight) * jnp.cos(travel)
-    sine = jnp.asarray(weight) * jnp.sin(travel)
-    turned = jnp.where(jnp.asarray(mode == 0), jnp.cos(-math.pi * bulk_shift[0]) / total, cosine)
-    aux = jnp.concatenate(
-        [
-            jnp.stack([jnp.asarray(square), jnp.asarray(ends), cosine, sine, turned]),
-            jnp.broadcast_to(diffusivity[:, None], (field_count, half)),
-        ]
-    )
+    late = np.where(mode == 0, np.float32(np.pi), wave).astype(np.float32)
+    blank = np.zeros_like(wave)
+    aux = np.stack([square, ends, wave, late, weight, blank, blank, blank])
     table = real_table(total)
     high = table.astype(jnp.bfloat16)
     low = (table - high.astype(np.float32)).astype(jnp.bfloat16)
     piece = (field_count, gx_count, own_rows, slab_width)
     vmem = pl.BlockSpec(memory_space=pltpu.VMEM)
     hbm = pl.BlockSpec(memory_space=pl.ANY)
+    smem = pl.BlockSpec(memory_space=pltpu.SMEM)
     links = field_count // 2 * gx_count
+    drops = drop_cell.shape[0]
     out = pl.pallas_call(
         functools.partial(step_kernel, gx_count, gz_count),
         out_shape=jax.ShapeDtypeStruct((field_count, row_count, slab_width), jnp.float32),
-        in_specs=[vmem] * 6 + [hbm] * 2,
+        in_specs=[vmem] * 5 + [smem] * 2 + [hbm] * 5,
         out_specs=vmem,
         scratch_shapes=[
+            pltpu.VMEM((field_count, row_count, slab_width), jnp.float32),
+            pltpu.VMEM((row_count, row_count), jnp.float32),
+            pltpu.VMEM((row_count, row_count), jnp.float32),
+            pltpu.VMEM((4, drops), jnp.float32),
             pltpu.VMEM((total, total), jnp.bfloat16),
             pltpu.VMEM((total, total), jnp.bfloat16),
             pltpu.VMEM((row_count, 3 * row_count), jnp.bfloat16),
-            pltpu.VMEM((gz_count,) + drops.shape, jnp.float32),
+            pltpu.VMEM((gz_count, 4, drops), jnp.float32),
             pltpu.VMEM((row_count, 4 * slab_width), jnp.float32),
             pltpu.VMEM(piece, jnp.float32),
             pltpu.VMEM(piece, jnp.float32),
@@ -296,18 +311,22 @@
             pltpu.SemaphoreType.DMA((links,)),
             pltpu.SemaphoreType.DMA((links,)),
             pltpu.SemaphoreType.DMA((links,)),
-            pltpu.SemaphoreType.DMA((2,)),
+            pltpu.SemaphoreType.DMA((5,)),
         ],
         compiler_params=pltpu.CompilerParams(
-            collective_id=0, has_side_effects=True, vmem_limit_bytes=48 * 2**20
+            collective_id=0, has_side_effects=True, vmem_limit_bytes=62 * 2**20
         ),
     )(
+        drop_cell[None],
+        drop_plane[None],
+        drop_rate,
+        wall_eigen[None],
+        jnp.asarray(aux),
+        diffusivity,
+        bulk_shift,
         field.reshape(field_count, row_count, slab_width),
-        drops,
         dual_part,
         basis_part,
-        wall_eigen[:, None],
-        aux,
         jnp.asarray(high),
         jnp.asarray(low),
     )

time: 67.6 us -> 61.3 us (0.907)
  local copies, waits for them, and re-layouts: 7.01 us -> 2.26 us
  other arithmetic: 3.01 us -> 0 us
  Pallas kernels: 56.3 us -> 58.1 us
    unnamed x7 -> x1, local copies, waits for them, and re-layouts: 4.64 us -> 2.26 us
    pallas_call x1, Pallas kernels: 56.3 us -> 58.1 us  [dense_step(): pl.pallas_call(functools.partial(step_kernel, gx_count, gz_count), out_sh...]
    broadcast_in_dim x2 -> x0, local copies, waits for them, and re-layouts: 1.55 us -> none  [the longest x1 0.82 us: dense_step(): wall_eigen[:, None]]
    convert_element_type x2 -> x0, other arithmetic: 1.44 us -> none  [the longest x1 0.72 us: dense_step(): drop_cell.astype(jnp.float32)[None]]
    concatenate x1 -> x0, local copies, waits for them, and re-layouts: 0.82 us -> none  [dense_step(): jnp.concatenate([jnp.stack([jnp.asarray(square), jnp.asarray(ends), cosin...]
    concatenate x1 -> x0, other arithmetic: 0.81 us -> none  [dense_step(): jnp.concatenate([drop_cell.astype(jnp.float32)[None], drop_plane.astype(j...]
    select_n x1 -> x0, other arithmetic: 0.76 us -> none  [dense_step(): jnp.where(jnp.asarray(mode == 0), jnp.cos(-math.pi * bulk_shift[0]) / tot...]
where the time goes in v3:
time: 61.3 us; the launch traced here: 61 us
  Pallas kernels  58.1 us (95%)
  local copies, waits for them, and re-layouts  2.26 us (4%)
  between operations  0.66 us (1%)
    pallas_call x1, Pallas kernels, dense_step(): pl.pallas_call(functools.partial(step_kernel, gx_count, gz_count), out_sh...  58.1 us
    unnamed x1, local copies, waits for them, and re-layouts  2.26 us

profile of v3, /device:TPU:13, one launch (start us, length us, event | category | flops | bytes accessed | tf_op | source)
XLA Modules:
  0.0 61.0 jit_solution(9222967270673349961)
XLA Ops:
  0.7 58.1 %shard_map.118 = f32[4,512,128]{2,1,0:T(8,128)} custom-call(s32[1,4096]{1,0:T(1,128)} %bitcast.9, s32[1,4096]{1,0:T(1,128)} %bitcast.10, f32[2,4096]{1,0:T(2,128)} %rate_ref.1, f32[1,512]{1,0:T(1,128)} %bitcast.11, f32[8,512]{1,0:T(8,128)} %constant.6.clone.aux_ref, f32[4]{0:T(128)} %diffusivity_ref.1, f32[1]{0:T(128)S(6)} %copy.15.shift_ref, ...), custom_call_target="tpu_custom_call" | custom-call | tf_op jit(solution)/shard_map/pallas_call | solution.py:289
  58.8 2.3 %copy.16 = f32[4,1,512,128]{3,2,1,0:T(8,128)} copy(f32[4,1,512,128]{3,2,1,0:T(8,128)} %bitcast.7) | data formatting | bytes 2097152

commit v4 on v3

--- a/solution.py
+++ b/solution.py
@@ -133,7 +133,7 @@
 
     def exchange(pair, source, landing, send_sem, recv_sem):
         copies = []
-        for off in range(1, gx_count):
+        for off in sorted(range(1, gx_count), key=lambda step: abs(2 * step - gx_count)):
             target = lax.rem(me + off, gx_count)
             copy = pltpu.make_async_remote_copy(
                 src_ref=source.at[pl.ds(2 * pair, 2), target],
@@ -164,7 +164,7 @@
     gathered[0] = drop_ref[...]
     total_ref[...] = jnp.zeros_like(total_ref)
     for copy in drop_copies:
-        copy.wait()
+        copy.wait_recv()
     drops = drop_ref.shape[1]
     block = min(2048, drops)
     blocks = drops // block
@@ -226,7 +226,7 @@
         sine = damps[0] * sin_row
         turned = damps[1] * turned_row
         for copy in first[pair]:
-            copy.wait()
+            copy.wait_recv()
         rows = jnp.concatenate(
             [
                 recv_one[2 * pair : 2 * pair + 2, slab].reshape(2 * own_rows, slab_width)
@@ -249,7 +249,7 @@
         second.append(exchange(pair, send_two, recv_two, two_send, two_recv))
     for pair in range(pairs):
         for copy in second[pair]:
-            copy.wait()
+            copy.wait_recv()
         values = apply_matrix(
             jnp.concatenate(
                 [recv_two[2 * pair + side].reshape(row_count, slab_width) for side in range(2)],
@@ -258,6 +258,8 @@
         )
         for side in range(2):
             out_ref[2 * pair + side] = values[:, side * slab_width : (side + 1) * slab_width]
+    for copy in drop_copies + first[0] + first[1] + second[0] + second[1]:
+        copy.wait_send()
 
 
 def dense_step(

time: 61.3 us -> 61.2 us (level)
  no operation moved by 1% of the time
where the time goes in v4:
time: 61.2 us; the launch traced here: 61 us
  Pallas kernels  58.1 us (95%)
  local copies, waits for them, and re-layouts  2.26 us (4%)
  between operations  0.66 us (1%)
    pallas_call x1, Pallas kernels, dense_step(): pl.pallas_call(functools.partial(step_kernel, gx_count, gz_count), out_sh...  58.1 us
    unnamed x1, local copies, waits for them, and re-layouts  2.26 us

profile of v4, /device:TPU:13, one launch (start us, length us, event | category | flops | bytes accessed | tf_op | source)
XLA Modules:
  0.0 61.0 jit_solution(1029759760759205912)
XLA Ops:
  0.7 58.1 %shard_map.118 = f32[4,512,128]{2,1,0:T(8,128)} custom-call(s32[1,4096]{1,0:T(1,128)} %bitcast.9, s32[1,4096]{1,0:T(1,128)} %bitcast.10, f32[2,4096]{1,0:T(2,128)} %rate_ref.1, f32[1,512]{1,0:T(1,128)} %bitcast.11, f32[8,512]{1,0:T(8,128)} %constant.6.clone.aux_ref, f32[4]{0:T(128)} %diffusivity_ref.1, f32[1]{0:T(128)S(6)} %copy.15.shift_ref, ...), custom_call_target="tpu_custom_call" | custom-call | tf_op jit(solution)/shard_map/pallas_call | solution.py:291
  58.7 2.3 %copy.16 = f32[4,1,512,128]{3,2,1,0:T(8,128)} copy(f32[4,1,512,128]{3,2,1,0:T(8,128)} %bitcast.7) | data formatting | bytes 2097152

commit v5 on v3

--- a/solution.py
+++ b/solution.py
@@ -166,7 +166,7 @@
     for copy in drop_copies:
         copy.wait()
     drops = drop_ref.shape[1]
-    block = min(2048, drops)
+    block = min(4096, drops)
     blocks = drops // block
 
     def deposit(step, carry):

time: 61.3 us -> 60.4 us (0.985)
  Pallas kernels: 58.1 us -> 57.3 us
    pallas_call x1, Pallas kernels: 58.1 us -> 57.3 us  [dense_step(): pl.pallas_call(functools.partial(step_kernel, gx_count, gz_count), out_sh...]
where the time goes in v5:
time: 60.4 us; the launch traced here: 60.2 us
  Pallas kernels  57.3 us (95%)
  local copies, waits for them, and re-layouts  2.26 us (4%)
  between operations  0.66 us (1%)
    pallas_call x1, Pallas kernels, dense_step(): pl.pallas_call(functools.partial(step_kernel, gx_count, gz_count), out_sh...  57.3 us
    unnamed x1, local copies, waits for them, and re-layouts  2.26 us

profile of v5, /device:TPU:13, one launch (start us, length us, event | category | flops | bytes accessed | tf_op | source)
XLA Modules:
  0.0 60.2 jit_solution(9430036052841360922)
XLA Ops:
  0.7 57.3 %shard_map.118 = f32[4,512,128]{2,1,0:T(8,128)} custom-call(s32[1,4096]{1,0:T(1,128)} %bitcast.9, s32[1,4096]{1,0:T(1,128)} %bitcast.10, f32[2,4096]{1,0:T(2,128)} %rate_ref.1, f32[1,512]{1,0:T(1,128)} %bitcast.11, f32[8,512]{1,0:T(8,128)} %constant.6.clone.aux_ref, f32[4]{0:T(128)} %diffusivity_ref.1, f32[1]{0:T(128)S(6)} %copy.15.shift_ref, ...), custom_call_target="tpu_custom_call" | custom-call | tf_op jit(solution)/shard_map/pallas_call | solution.py:289
  57.9 2.3 %copy.16 = f32[4,1,512,128]{3,2,1,0:T(8,128)} copy(f32[4,1,512,128]{3,2,1,0:T(8,128)} %bitcast.7) | data formatting | bytes 2097152
